TPU v7x, 512 devices: a whole 4x8x8 slice. The times are simulated.
512 devices in a mesh: rec: 16 (over z, core), frame: 32 (over x, y).
Axes of the slice: x: 4, y: 8, z: 8, core: 2. Of those that a mesh axis runs over, the one named last changes fastest.
Arguments:
- frames: bfloat16 [16, 49152, 256], P('rec', 'frame'), may hold values from -10 to 10
- texts: bfloat16 [32, 224, 256], P('rec', 'frame'), may hold values from -100 to 100
- pair_rec: int32 [32, 1], replicated, may hold values from 0 to 15, as said below
- pair_text: int32 [32], replicated, may hold values from 0 to 31, as said below
- pair_label: int32 [32], replicated, may hold values 0 or 1
Outputs:
- loss: float32 [], replicated
- grad_frames: bfloat16 [16, 49152, 256], P('rec', 'frame')
- grad_texts: bfloat16 [32, 224, 256], P('rec', 'frame')
Inputs may be any that keep to these rules, and one draw needn't show every extreme that they name: `pair_rec`: no recording is named by more than 6 pairs, some recording by exactly 6, and every recording by at least one. A pair's text is held by the index of rec one after, one before, or 8 after its recording (counted round): pair_text // 2 = (pair_rec + k) mod 16 with k one of 1, 15, 8.
All inputs are finite; a program needn't handle non-finite values.
Results may differ from a plain program's by a relative error of at most 0.0085.
Values may be sent and summed in bfloat16 or wider, within the bound.
A program may use at most 64 MiB of HBM per device.

v0:
```python
import jax
import jax.numpy as jnp
from jax import lax
from jax.sharding import PartitionSpec as P

MOST = 6
EPS = 1e-06
TEMP = 10.0
BIAS = -1.0
LOSS_SCALE = 2048.0


def slot_tables(pair_rec, pair_text, pair_label, here, most):
    record = pair_rec[:, 0]
    count = record.shape[0]
    order = jnp.arange(count, dtype=jnp.int32)
    same = (record[:, None] == record[None, :]).astype(jnp.int32)
    earlier = (order[None, :] < order[:, None]).astype(jnp.int32)
    rank = jnp.sum(same * earlier, axis=1)
    places = jnp.arange(most, dtype=jnp.int32)
    chosen = ((record[None, :] == here) & (rank[None, :] == places[:, None])).astype(jnp.int32)
    valid = jnp.sum(chosen, axis=1)
    slot_text = jnp.sum(chosen * pair_text[None, :], axis=1)
    sign = jnp.sum(chosen * (2 * pair_label[None, :] - 1), axis=1)
    return (valid, slot_text, sign)


def pair_terms(score, valid, sign, tokens):
    margin = -sign * (TEMP * score + BIAS)
    loss_part = valid * jax.nn.softplus(margin)
    grad_cos = -LOSS_SCALE * TEMP * valid * sign * jax.nn.sigmoid(margin) / tokens
    return (loss_part, grad_cos)


def body(frames, texts, pair_rec, pair_text, pair_label):
    here = lax.axis_index("rec")
    part = lax.axis_index("frame")
    owned, width_rows, width = texts.shape
    tokens = width_rows * lax.axis_size("frame")
    n_text = owned * lax.axis_size("rec")
    valid, slot_text, sign = slot_tables(pair_rec, pair_text, pair_label, here, MOST)
    valid_f = valid.astype(jnp.float32)
    sign_f = sign.astype(jnp.float32)
    picks = (
        (slot_text[:, None] == jnp.arange(n_text, dtype=jnp.int32)[None, :]) & (valid[:, None] > 0)
    ).astype(jnp.bfloat16)
    whole = lax.all_gather(texts, "frame", axis=1, tiled=True)
    query_vectors = jnp.einsum(
        "jc,cgx->jgx",
        picks,
        lax.all_gather(whole, "rec", axis=0, tiled=True),
        preferred_element_type=jnp.float32,
    ).astype(jnp.bfloat16)
    upstream_signal = frames[0]
    logit_scale = width ** (-0.5)
    pair_scores = (
        jnp.einsum(
            "ype,je->ypj", query_vectors, upstream_signal, preferred_element_type=jnp.float32
        )
        * logit_scale
    )
    local_max = jnp.max(pair_scores, axis=2)
    row_max = lax.pmax(local_max, "frame")
    expo = jnp.exp(pair_scores - row_max[..., None])
    batch_weights = expo.astype(jnp.bfloat16)
    value_partial = jnp.einsum(
        "pqx,xh->pqh", batch_weights, upstream_signal, preferred_element_type=jnp.float32
    )
    query_f = query_vectors.astype(jnp.float32)
    q_norm = lax.rsqrt(jnp.sum(query_f * query_f, axis=2) + EPS)
    q_unit = query_f * q_norm[..., None]
    context = lax.psum(value_partial, "frame")
    c_norm = lax.rsqrt(jnp.sum(context * context, axis=2) + EPS)
    c_unit = context * c_norm[..., None]
    cos = jnp.sum(q_unit * c_unit, axis=2)
    score = jnp.mean(cos, axis=1)
    loss_part, grad_cos = pair_terms(score, valid_f, sign_f, tokens)
    weight = grad_cos[:, None, None]
    d_context = weight * (q_unit - cos[..., None] * c_unit) * c_norm[..., None]
    direct = weight * (c_unit - cos[..., None] * q_unit) * q_norm[..., None]
    direct_own = lax.dynamic_slice_in_dim(direct, part * width_rows, width_rows, 1)
    context_batch_gradient = d_context.astype(jnp.bfloat16)
    weight_gradient = jnp.einsum(
        "ype,je->ypj", context_batch_gradient, upstream_signal, preferred_element_type=jnp.float32
    )
    score_gradient = (expo * weight_gradient * logit_scale).astype(jnp.bfloat16)
    d_query = lax.psum_scatter(
        jnp.einsum(
            "slf,fd->lsd", score_gradient, upstream_signal, preferred_element_type=jnp.float32
        ),
        "frame",
        scatter_dimension=0,
        tiled=True,
    )
    d_query = d_query + jnp.transpose(direct_own, (1, 0, 2))
    text_term = jnp.einsum(
        "st,lsd->tld", picks.astype(jnp.float32), d_query, precision=lax.Precision.HIGHEST
    )
    grad_texts = lax.psum_scatter(text_term, "rec", scatter_dimension=0, tiled=True).astype(
        jnp.bfloat16
    )
    frame_loss_piece = jnp.einsum(
        "cvm,cvz->mz", score_gradient, query_vectors, preferred_element_type=jnp.float32
    )
    frame_loss_piece = frame_loss_piece + jnp.einsum(
        "cvm,cvz->mz", batch_weights, context_batch_gradient, preferred_element_type=jnp.float32
    )
    grad_frames = frame_loss_piece.astype(jnp.bfloat16)[None]
    loss = lax.psum(jnp.sum(loss_part), "rec")
    return (loss, grad_frames, grad_texts)


def solution(mesh):
    return jax.shard_map(
        body,
        mesh=mesh,
        in_specs=(P("rec", "frame", None), P("rec", "frame", None), P(), P(), P()),
        out_specs=(P(), P("rec", "frame", None), P("rec", "frame", None)),
        check_vma=False,
    )
```

profile of v0, /device:TPU:16, one launch (start us, length us, event | category | flops | bytes accessed | tf_op | source)
XLA Modules:
  0.0 644.4 jit_solution(15901261809968272552)
XLA Ops:
  7.2 49.8 %all_gather.6 = bf16[2,224,256]{2,0,1:T(2,128)(2,1)S(1)} all-gather(bf16[2,7,256]{2,0,1:T(2,128)(2,1)} %param.6), channel_id=1, replica_groups=mesh['rec'=16,'frame'=32] {'frame'}, dimensions={1}, use_global_device_ids=true | all-gather | bytes 236544 | tf_op jit(solution)/shard_map/all_gather | solution.py:47
  57.0 0.7 copy.20
  57.8 0.9 select_reduce_fusion
  60.1 1.3 select_reduce_fusion.2
  61.4 43.4 %all-gather.2.cloned.1.call-done = bf16[32,224,256]{2,1,0:T(8,128)(2,1)} async-done(((bf16[2,224,256]{2,1,0:T(8,128)(2,1)}), bf16[32,224,256]{2,1,0:T(8,128)(2,1)}) %all-gather.2.cloned.1.call-update) | async-done | bytes 3670032 | tf_op jit(solution)/shard_map/all_gather | solution.py:51
  104.7 4.3 fusion.6
  109.0 4.4 multiply_reduce_fusion
  113.4 71.4 %pmax.7 = f32[6,224]{1,0:T(8,128)S(1)} all-reduce(f32[6,224]{1,0:T(8,128)S(1)} %get-tuple-element.17), channel_id=1, replica_groups=mesh['rec'=16,'frame'=32] {'frame'}, use_global_device_ids=true, to_apply=%region_6.0 | all-reduce | flops 1344 | bytes 10752 | tf_op jit(solution)/shard_map/pmax | solution.py:63
  184.8 4.9 fusion.13
  189.7 2.1 copy.23
  192.6 157.1 %all-reduce.5.cloned.1.call-done = f32[6,224,256]{2,0,1:T(8,128)} async-done(((f32[6,224,256]{2,0,1:T(8,128)}), f32[6,224,256]{2,0,1:T(8,128)}) %all-reduce.5.cloned.1.call-update) | async-done | bytes 1376272 | tf_op jit(solution)/shard_map/psum | solution.py:72
  349.7 1.9 multiply_reduce_fusion.1
  351.6 2.4 multiply_reduce_fusion.2
  354.0 1.4 fusion.44
  355.4 1.8 convert_multiply_fusion
  357.2 4.9 multiply_convert_fusion
  362.2 1.3 fusion.10
  364.2 2.1 copy.47
  366.2 1.3 dynamic-slice
  369.6 5.7 convolution_bitcast_fusion
  375.3 2.3 fusion.5
  377.6 209.2 %reduce-scatter.3.cloned.1.call-done = f32[7,6,256]{2,1,0:T(8,128)} async-done(((f32[224,6,256]{2,1,0:T(8,128)}), f32[7,6,256]{2,1,0:T(8,128)}) %reduce-scatter.3.cloned.1.call-update) | async-done | bytes 43024 | tf_op jit(solution)/shard_map/reduce_scatter | solution.py:87
  586.9 1.3 fusion.27
  588.2 49.1 %all-reduce.6 = (f32[]{:T(128)}, bf16[32,7,256]{2,0,1:T(8,128)(2,1)S(1)}) all-reduce(f32[]{:T(128)} %get-tuple-element.14, f32[32,7,256]{2,0,1:T(8,128)S(1)} %fusion.27), channel_id=1, replica_groups=mesh['rec'=16,'frame'=32] {'rec'}, use_global_device_ids=true, to_apply=%region_11.12 | all-reduce | flops 57345 | bytes 344072 | tf_op jit(solution)/shard_map/psum | solution.py:109
  (38 shorter events, 5.2 us)
Async XLA Ops:
  7.2 101.8 %copy-start = (bf16[1,1536,256]{2,1,0:T(8,128)(2,1)S(1)}, bf16[1,1536,256]{2,1,0:T(8,128)(2,1)}, u32[]{:S(2)}) copy-start(bf16[1,1536,256]{2,1,0:T(8,128)(2,1)} %param.5) | copy-start | bytes 2359300
  7.2 97.5 %all-gather.2.cloned.1.call-start = ((), (), s32[]{:S(2)}) async-start(), calls=%async_computation.1 | async-start | bytes 3899392 | tf_op jit(solution)/shard_map/all_gather | solution.py:51
  57.8 291.9 %all-reduce.5.cloned.1.call-start = ((), (), s32[]{:S(2)}) async-start(), calls=%async_computation.2 | async-start | bytes 3670016 | tf_op jit(solution)/shard_map/psum | solution.py:72
  61.3 43.4 %copy-start.9 = (s32[6]{0:T(128)}, s32[6]{0:T(128)S(1)}, u32[]{:S(2)}) copy-start(s32[6]{0:T(128)S(1)} %get-tuple-element.7) | copy-start | bytes 76
  61.3 47.6 %copy-start.4 = (s32[6]{0:T(128)}, s32[6]{0:T(128)S(1)}, u32[]{:S(2)}) copy-start(s32[6]{0:T(128)S(1)} %get-tuple-element.6) | copy-start | bytes 76
  61.4 47.6 %copy-start.8 = (pred[6]{0:T(512)(128)(4,1)}, pred[6]{0:T(512)(128)(4,1)S(1)}, u32[]{:S(2)}) copy-start(pred[6]{0:T(512)(128)(4,1)S(1)} %broadcast_compare_fusion) | copy-start | bytes 22
  191.8 395.1 %reduce-scatter.3.cloned.1.call-start = ((), (), s32[]{:S(2)}) async-start(), calls=%async_computation.3 | async-start | bytes 1892352 | tf_op jit(solution)/shard_map/reduce_scatter | solution.py:87
  349.7 5.7 copy-start.1
  354.0 3.2 copy-start.3
  355.4 6.8 %copy-start.6 = (f32[6]{0:T(128)}, f32[6]{0:T(128)S(1)}, u32[]{:S(2)}) copy-start(f32[6]{0:T(128)S(1)} %get-tuple-element.13) | copy-start | bytes 76
  357.2 5.0 copy-start.2
  362.2 2.0 copy-start.10
  369.6 5.7 copy-start.11
  375.3 211.6 %copy-start.5 = (s32[6]{0:T(128)S(1)}, s32[6]{0:T(128)}, u32[]{:S(2)}) copy-start(s32[6]{0:T(128)} %copy-done.4) | copy-start | bytes 76
  375.3 211.6 %copy-start.7 = (f32[6]{0:T(128)S(1)}, f32[6]{0:T(128)}, u32[]{:S(2)}) copy-start(f32[6]{0:T(128)} %copy-done.6) | copy-start | bytes 76
Sparse Core Ops, SparseCore 0:
  57.9 46.7 all-gather.1
  191.9 157.7 all-reduce.4
  366.4 220.4 reduce-scatter.2
where the time goes:
time: 645 us; the launch traced here: 644 us
  waiting for transfers between devices  410 us (64%)
  blocking collectives  170 us (26%)
  matrix products  29 us (4%)
  between operations  14.6 us (2%)
  other arithmetic  11.7 us (2%)
  local copies, waits for them, and re-layouts  8.88 us (1%)
    reduce_scatter x1, waiting for transfers between devices, body(): lax.psum_scatter(jnp.einsum('slf,fd->lsd', score_gradient, upstream_signa...  209 us
    psum x1, waiting for transfers between devices, body(): context = lax.psum(value_partial, 'frame')  157 us
    pmax x1, blocking collectives, body(): row_max = lax.pmax(local_max, 'frame')  71.4 us
    all_gather x1, blocking collectives, body(): whole = lax.all_gather(texts, 'frame', axis=1, tiled=True)  49.8 us
    psum x1, blocking collectives, body(): loss = lax.psum(jnp.sum(loss_part), 'rec')  49.1 us
    all_gather x1, waiting for transfers between devices, body(): lax.all_gather(whole, 'rec', axis=0, tiled=True)  43.4 us
  transfers between devices with their start and end apart: 3, of which 3 were waited for; matrix products, arithmetic and copies ran while one was open for 2% of the time, Pallas kernels for 0%

commit v1 on v0

--- a/solution.py
+++ b/solution.py
@@ -8,6 +8,15 @@
 TEMP = 10.0
 BIAS = -1.0
 LOSS_SCALE = 2048.0
+
+
+def do_group(mat):
+    seen = []
+    for _ in range(lax.axis_size("rec")):
+        seen.append(mat)
+    wide_out = jnp.stack(seen)
+    res = jnp.concatenate(lax.all_to_all(wide_out, axis_name="rec", split_axis=0, concat_axis=0), 0)
+    return res
 
 
 def slot_tables(pair_rec, pair_text, pair_label, here, most):
@@ -46,10 +55,7 @@
     ).astype(jnp.bfloat16)
     whole = lax.all_gather(texts, "frame", axis=1, tiled=True)
     query_vectors = jnp.einsum(
-        "jc,cgx->jgx",
-        picks,
-        lax.all_gather(whole, "rec", axis=0, tiled=True),
-        preferred_element_type=jnp.float32,
+        "jc,cgx->jgx", picks, do_group(whole), preferred_element_type=jnp.float32
     ).astype(jnp.bfloat16)
     upstream_signal = frames[0]
     logit_scale = width ** (-0.5)

time: 645 us -> 708 us (1.098)
  waiting for transfers between devices: 410 us -> 448 us
  local copies, waits for them, and re-layouts: 8.88 us -> 28 us
  starting transfers between devices: 0.3 us -> 10.9 us
    all_to_all x0 -> x1, waiting for transfers between devices: none -> 81.7 us  [do_group(): lax.all_to_all(wide_out, axis_name='rec', split_axis=0, concat_axis=0)]
    all_gather x1 -> x0, waiting for transfers between devices: 43.4 us -> none  [body(): lax.all_gather(whole, 'rec', axis=0, tiled=True)]
    all_to_all x0 -> x1, starting transfers between devices: none -> 10.6 us  [do_group(): lax.all_to_all(wide_out, axis_name='rec', split_axis=0, concat_axis=0)]
    all_to_all x0 -> x1, local copies, waits for them, and re-layouts: none -> 8.06 us  [do_group(): lax.all_to_all(wide_out, axis_name='rec', split_axis=0, concat_axis=0)]
where the time goes in v1:
time: 708 us; the launch traced here: 707 us
  waiting for transfers between devices  448 us (63%)
  blocking collectives  168 us (24%)
  local copies, waits for them, and re-layouts  28 us (4%)
  matrix products  27.6 us (4%)
  between operations  14.9 us (2%)
  starting transfers between devices  10.9 us (2%)
  other arithmetic  8.97 us (1%)
    reduce_scatter x1, waiting for transfers between devices, body(): lax.psum_scatter(jnp.einsum('slf,fd->lsd', score_gradient, upstream_signa...  209 us
    psum x1, waiting for transfers between devices, body(): context = lax.psum(value_partial, 'frame')  158 us
    all_to_all x1, waiting for transfers between devices, do_group(): lax.all_to_all(wide_out, axis_name='rec', split_axis=0, concat_axis=0)  81.7 us
    pmax x1, blocking collectives, body(): row_max = lax.pmax(local_max, 'frame')  69.3 us
    all_gather x1, blocking collectives, body(): whole = lax.all_gather(texts, 'frame', axis=1, tiled=True)  49.8 us
    psum x1, blocking collectives, body(): loss = lax.psum(jnp.sum(loss_part), 'rec')  49.1 us
  transfers between devices with their start and end apart: 3, of which 3 were waited for; matrix products, arithmetic and copies ran while one was open for 2% of the time, Pallas kernels for 0%

profile of v1, /device:TPU:16, one launch (start us, length us, event | category | flops | bytes accessed | tf_op | source)
XLA Modules:
  0.0 706.9 jit_solution(3332339999999266186)
XLA Ops:
  7.2 49.8 %all_gather.3 = bf16[2,224,256]{2,0,1:T(2,128)(2,1)S(1)} all-gather(bf16[2,7,256]{2,0,1:T(2,128)(2,1)} %param.6), channel_id=1, replica_groups=mesh['rec'=16,'frame'=32] {'frame'}, dimensions={1}, use_global_device_ids=true | all-gather | bytes 236544 | tf_op jit(solution)/shard_map/all_gather | solution.py:56
  57.0 4.7 stack.2
  61.7 10.6 %all-to-all-start = ((bf16[16,2,224,256]{3,1,2,0:T(2,128)(2,1)}), bf16[16,2,224,256]{3,1,2,0:T(2,128)(2,1)}, u32[]{:S(2)}, u32[]{:S(2)}) async-start(bf16[16,2,224,256]{3,1,2,0:T(2,128)(2,1)} %stack.2), calls=%async_computation | async-start | bytes 7340032 | tf_op jit(solution)/shard_map/all_to_all | solution.py:18
  73.7 81.7 %all-to-all-done = bf16[16,2,224,256]{3,1,2,0:T(2,128)(2,1)} async-done(((bf16[16,2,224,256]{3,1,2,0:T(2,128)(2,1)}), bf16[16,2,224,256]{3,1,2,0:T(2,128)(2,1)}, u32[]{:S(2)}, u32[]{:S(2)}) %all-to-all-start) | async-done | bytes 3670048 | tf_op jit(solution)/shard_map/all_to_all | solution.py:18
  155.4 8.1 %copy.19 = bf16[16,2,224,256]{3,1,0,2:T(2,128)(2,1)} copy(bf16[16,2,224,256]{3,1,2,0:T(2,128)(2,1)} %all-to-all-done) | data formatting | bytes 7340032 | tf_op jit(solution)/shard_map/all_to_all | solution.py:18
  163.4 6.6 reshape.59
  170.0 2.8 fusion.4
  172.8 4.4 multiply_reduce_fusion
  177.2 69.3 %pmax.7 = f32[6,224]{1,0:T(8,128)S(1)} all-reduce(f32[6,224]{1,0:T(8,128)S(1)} %get-tuple-element.17), channel_id=1, replica_groups=mesh['rec'=16,'frame'=32] {'frame'}, use_global_device_ids=true, to_apply=%region_6.0 | all-reduce | flops 1344 | bytes 10752 | tf_op jit(solution)/shard_map/pmax | solution.py:69
  246.6 4.9 fusion.8
  251.4 2.1 copy.21
  254.4 157.5 %all-reduce.5.cloned.1.call-done = f32[6,224,256]{2,0,1:T(8,128)} async-done(((f32[6,224,256]{2,0,1:T(8,128)}), f32[6,224,256]{2,0,1:T(8,128)}) %all-reduce.5.cloned.1.call-update) | async-done | bytes 1376272 | tf_op jit(solution)/shard_map/psum | solution.py:78
  412.0 1.9 multiply_reduce_fusion.1
  413.8 2.4 multiply_reduce_fusion.2
  416.3 1.4 fusion.39
  417.7 1.8 convert_multiply_fusion
  419.5 4.9 multiply_convert_fusion
  426.4 2.1 copy.39
  428.5 1.3 dynamic-slice
  431.8 5.7 convolution_bitcast_fusion
  437.5 2.3 fusion.3
  439.9 209.2 %reduce-scatter.3.cloned.1.call-done = f32[7,6,256]{2,1,0:T(8,128)} async-done(((f32[224,6,256]{2,1,0:T(8,128)}), f32[7,6,256]{2,1,0:T(8,128)}) %reduce-scatter.3.cloned.1.call-update) | async-done | bytes 43024 | tf_op jit(solution)/shard_map/reduce_scatter | solution.py:93
  649.1 1.3 fusion.22
  650.4 49.1 %all-reduce.6 = (f32[]{:T(128)}, bf16[32,7,256]{2,0,1:T(8,128)(2,1)S(1)}) all-reduce(f32[]{:T(128)} %get-tuple-element.14, f32[32,7,256]{2,0,1:T(8,128)S(1)} %fusion.22), channel_id=1, replica_groups=mesh['rec'=16,'frame'=32] {'rec'}, use_global_device_ids=true, to_apply=%region_11.12 | all-reduce | flops 57345 | bytes 344072 | tf_op jit(solution)/shard_map/psum | solution.py:115
  (45 shorter events, 6.4 us)
Async XLA Ops:
  7.2 165.6 %copy-start = (bf16[1,1536,256]{2,1,0:T(8,128)(2,1)S(1)}, bf16[1,1536,256]{2,1,0:T(8,128)(2,1)}, u32[]{:S(2)}) copy-start(bf16[1,1536,256]{2,1,0:T(8,128)(2,1)} %param.5) | copy-start | bytes 2359300
  61.7 10.7 %copy-start.11 = (s32[32,1]{0,1:T(1,128)S(1)}, s32[32,1]{0,1:T(1,128)}, u32[]{:S(2)}) copy-start(s32[32,1]{0,1:T(1,128)} %param.7) | copy-start | bytes 388
  61.7 10.9 %copy-start.12 = (s32[32]{0:T(128)S(1)}, s32[32]{0:T(128)}, u32[]{:S(2)}) copy-start(s32[32]{0:T(128)} %param.9) | copy-start | bytes 388
  61.7 10.9 %copy-start.10 = (s32[32]{0:T(128)S(1)}, s32[32]{0:T(128)}, u32[]{:S(2)}) copy-start(s32[32]{0:T(128)} %param.8) | copy-start | bytes 388
  61.7 93.7 %all-to-all-start = ((bf16[16,2,224,256]{3,1,2,0:T(2,128)(2,1)}), bf16[16,2,224,256]{3,1,2,0:T(2,128)(2,1)}, u32[]{:S(2)}, u32[]{:S(2)}) async-start(bf16[16,2,224,256]{3,1,2,0:T(2,128)(2,1)} %stack.2), calls=%async_computation | async-start | bytes 7340032 | tf_op jit(solution)/shard_map/all_to_all | solution.py:18
  72.3 339.7 %all-reduce.5.cloned.1.call-start = ((), (), s32[]{:S(2)}) async-start(), calls=%async_computation.2 | async-start | bytes 3670016 | tf_op jit(solution)/shard_map/psum | solution.py:78
  73.2 0.5 copy-start.9
  73.2 96.8 %copy-start.4 = (s32[6]{0:T(128)}, s32[6]{0:T(128)S(1)}, u32[]{:S(2)}) copy-start(s32[6]{0:T(128)S(1)} %get-tuple-element.6) | copy-start | bytes 76
  73.7 96.3 %copy-start.8 = (pred[6]{0:T(512)(128)(4,1)}, pred[6]{0:T(512)(128)(4,1)S(1)}, u32[]{:S(2)}) copy-start(pred[6]{0:T(512)(128)(4,1)S(1)} %broadcast_compare_fusion) | copy-start | bytes 22
  253.5 395.6 %reduce-scatter.3.cloned.1.call-start = ((), (), s32[]{:S(2)}) async-start(), calls=%async_computation.3 | async-start | bytes 1892352 | tf_op jit(solution)/shard_map/reduce_scatter | solution.py:93
  412.0 5.7 copy-start.1
  416.3 3.2 copy-start.3
  417.6 6.8 copy-start.6
  419.5 5.0 copy-start.2
  424.4 2.0 copy-start.13
  431.8 5.7 copy-start.14
  437.5 211.6 %copy-start.5 = (s32[6]{0:T(128)S(1)}, s32[6]{0:T(128)}, u32[]{:S(2)}) copy-start(s32[6]{0:T(128)} %copy-done.4) | copy-start | bytes 76
  437.5 211.6 %copy-start.7 = (f32[6]{0:T(128)S(1)}, f32[6]{0:T(128)}, u32[]{:S(2)}) copy-start(f32[6]{0:T(128)} %copy-done.6) | copy-start | bytes 76
Sparse Core Ops, SparseCore 0:
  253.6 158.2 all-reduce.4
  428.6 220.4 reduce-scatter.2
